TPU v7x, 32 devices: a whole 2x2x4 slice. The times are simulated.
32 devices in a mesh: lat: 4 (over x, core), lon: 8 (over z, y).
Axes of the slice: x: 2, y: 2, z: 4, core: 2. Of those that a mesh axis runs over, the one named last changes fastest.
Arguments:
- probe_signs: int32 [16, 1024, 512], P(None, 'lon', 'lat'), may hold values from -1 to 1, as said below
- ocean_mask: int32 [1024, 512], P('lon', 'lat'), may hold values 0 or 1
- kappa_sq: float32 [1024, 512], P('lon', 'lat'), may hold values from 0.02 to 0.5
- block_ids: int32 [1024, 512], P('lon', 'lat'), may hold values from 0 to 63
Outputs:
- solution: float32 [16, 1024, 512], P(None, 'lon', 'lat')
- trace_terms: float32 [16, 1024, 512], P(None, 'lon', 'lat')
- traces: float32 [16, 64], replicated
Inputs may be any that keep to these rules, and one draw needn't show every extreme that they name: `probe_signs`: each entry is -1 or +1.
All inputs are finite; a program needn't handle non-finite values. No bound on the sum of `ocean_mask` on one device may be relied on, other than what follows from the above.
Results may differ from a plain program's by a relative error of at most 0.0003.
Values sent between devices are 32-bit elements; how exact they have to be, the bound alone decides.
A program may use at most 64 MiB of HBM per device.

v0:
```python
import jax
import jax.numpy as jnp
from jax import lax
from jax.sharding import PartitionSpec as P

NB = 64
WIDTH = 5
SHIFTS = (0.2, 0.4)
FLOOR = 1e-6


def extended(cells, axis, dim, width, closed):
    count = lax.axis_size(axis)
    ends = count if closed else count - 1
    head = lax.slice_in_dim(cells, 0, width, axis=dim)
    tail = lax.slice_in_dim(cells, cells.shape[dim] - width, cells.shape[dim], axis=dim)
    before = lax.ppermute(tail, axis, [(i, (i + 1) % count) for i in range(ends)])
    after = lax.ppermute(head, axis, [((i + 1) % count, i) for i in range(ends)])
    return jnp.concatenate([before, cells, after], axis=dim)


def stencil(field, centre, side):
    total = field[:, :-2, 1:-1] + field[:, 2:, 1:-1]
    total = total + field[:, 1:-1, :-2] + field[:, 1:-1, 2:]
    return centre * field[:, 1:-1, 1:-1] - side * total


def weights(gram, right):
    g00, g01, g02, g11, g12, g22 = gram
    r0, r1, r2 = right
    l10 = g01 / g00
    l20 = g02 / g00
    d1 = g11 - l10 * g01
    e12 = g12 - l10 * g02
    ok1 = d1 > FLOOR * g11
    i1 = jnp.where(ok1, 1.0 / jnp.where(ok1, d1, 1.0), 0.0)
    l21 = e12 * i1
    d2 = g22 - l20 * g02 - l21 * e12
    ok2 = d2 > FLOOR * g22
    i2 = jnp.where(ok2, 1.0 / jnp.where(ok2, d2, 1.0), 0.0)
    z0 = r0
    z1 = r1 - l10 * z0
    z2 = r2 - l20 * z0 - l21 * z1
    y2 = z2 * i2
    y1 = z1 * i1 - l21 * y2
    y0 = z0 / g00 - l10 * y1 - l20 * y2
    return y0, y1, y2


def per_device(probe_signs, ocean_mask, kappa_sq, block_ids):
    probes = probe_signs.astype(jnp.float32) * ocean_mask.astype(jnp.float32)
    planes = jnp.concatenate([probes, kappa_sq[None]], axis=0)
    planes = extended(planes, "lon", 1, WIDTH, True)
    planes = extended(planes, "lat", 2, WIDTH, False)
    wide, wide_kappa = planes[:-1], planes[-1]
    ocean = wide[0] * wide[0]
    centre = ocean * (wide_kappa + 0.25)
    side = 0.0625 * ocean

    def cut(field, width):
        return field[..., width:field.shape[-2] - width, width:field.shape[-1] - width]

    v0 = wide
    w0 = stencil(v0, cut(centre, 1), cut(side, 1))
    v1 = stencil(w0, cut(centre, 2), cut(side, 2)) - SHIFTS[0] * cut(v0, 2)
    w1 = stencil(v1, cut(centre, 3), cut(side, 3))
    v2 = stencil(w1, cut(centre, 4), cut(side, 4)) - SHIFTS[1] * cut(v1, 2)
    w2 = stencil(v2, cut(centre, 5), cut(side, 5))
    v0, w0, v1, w1, v2 = (cut(f, n) for f, n in ((v0, 5), (w0, 4), (v1, 3), (w1, 2), (v2, 1)))

    def dot(a, b):
        return jnp.sum(a * b, axis=(1, 2))

    dots = jnp.stack([
        dot(w0, w0), dot(w0, w1), dot(w0, w2), dot(w1, w1), dot(w1, w2), dot(w2, w2),
        dot(v0, v0), dot(v0, v1), dot(v0, v2),
    ])
    terms = [kappa_sq * (v * w0 + w * v0) for v, w in ((v0, w0), (v1, w1), (v2, w2))]
    indicator = (
        block_ids[:, :, None] == jnp.arange(NB, dtype=jnp.int32)[None, None, :]
    ).astype(jnp.float32)
    sums = jnp.einsum(
        "szt,zti->si", jnp.concatenate(terms, axis=0), indicator, precision=lax.Precision.HIGHEST
    )
    count = probes.shape[0]
    both = jnp.concatenate([dots.reshape(-1), sums.reshape(-1)])
    both = lax.psum(both, ("lat", "lon"))
    dots = both[:9 * count].reshape(9, count)
    sums = both[9 * count:].reshape(3, count, NB)
    y = weights(tuple(dots[:6]), tuple(dots[6:]))
    yf = [a[:, None, None] for a in y]
    solved = yf[0] * v0 + yf[1] * v1 + yf[2] * v2
    trace = yf[0] * terms[0] + yf[1] * terms[1] + yf[2] * terms[2]
    cells_total = (
        kappa_sq.shape[0] * kappa_sq.shape[1] * lax.axis_size("lat") * lax.axis_size("lon")
    )
    traces = sum(a[:, None] * s for a, s in zip(y, sums)) / jnp.float32(cells_total // NB)
    return solved, trace, traces


def solution(mesh):
    placed = (P(None, "lon", "lat"), P("lon", "lat"), P("lon", "lat"), P("lon", "lat"))
    return jax.shard_map(
        per_device,
        mesh=mesh,
        in_specs=placed,
        out_specs=(P(None, "lon", "lat"), P(None, "lon", "lat"), P()),
        check_vma=False,
    )
```

profile of v0, /device:TPU:0, one launch (start us, length us, event | category | flops | bytes accessed | tf_op | source)
XLA Modules:
  0.0 105.5 jit_solution(7949228325773611590)
XLA Ops:
  0.6 0.0 copy-start.8
  0.6 1.8 %copy.29 = s32[16,128,128]{1,0,2:T(8,128)S(1)} copy(s32[16,128,128]{2,1,0:T(8,128)} %param.4) | data formatting | bytes 2097152 | tf_op args[0]
  2.4 0.8 convert_element_type.8
  3.3 0.1 copy.30
  3.4 0.0 copy-done.8
  3.4 0.1 copy.31
  3.5 0.1 convert_multiply_fusion
  3.6 2.2 %slice_maximum_fusion = (f32[17,5,128]{1,0,2:T(8,128)}, f32[17,5,128]{1,0,2:T(8,128)}) fusion(f32[1,128,128]{1,0,2:T(1,128)S(1)} %bitcast.16, f32[16,128,128]{1,0,2:T(8,128)S(1)} %convert_multiply_fusion), kind=kLoop, calls=%fused_computation.38 | loop fusion | flops 21760 | bytes 1201152 | tf_op jit(solution)/shard_map/concatenate | solution.py:52
  5.7 1.9 %copy.32 = f32[17,5,128]{2,0,1:T(8,128)S(1)} copy(f32[17,5,128]{1,0,2:T(8,128)} %get-tuple-element.36) | data formatting | bytes 87040 | tf_op jit(solution)/shard_map/slice | solution.py:16
  7.6 3.0 %collective-permute-start = (f32[17,5,128]{2,0,1:T(8,128)S(1)}, f32[17,5,128]{2,0,1:T(8,128)S(1)}, u32[]{:S(2)}, u32[]{:S(2)}) collective-permute-start(f32[17,5,128]{2,0,1:T(8,128)S(1)} %copy.32), channel_id=1, source_target_pairs={{0,1},{1,2},{2,3},{3,4},{4,5},{5,6},{6,7},{7,0},{8,9},{9,10},{10,1... | collective-permute-start | bytes 130568 | tf_op jit(solution)/shard_map/ppermute | solution.py:17
  10.6 1.9 %copy.33 = f32[17,5,128]{2,0,1:T(8,128)S(1)} copy(f32[17,5,128]{1,0,2:T(8,128)} %get-tuple-element.37) | data formatting | bytes 87040 | tf_op jit(solution)/shard_map/slice | solution.py:15
  12.5 3.1 %collective-permute-start.1 = (f32[17,5,128]{2,0,1:T(8,128)S(1)}, f32[17,5,128]{2,0,1:T(8,128)S(1)}, u32[]{:S(2)}, u32[]{:S(2)}) collective-permute-start(f32[17,5,128]{2,0,1:T(8,128)S(1)} %copy.33), channel_id=1, source_target_pairs={{1,0},{2,1},{3,2},{4,3},{5,4},{6,5},{7,6},{0,7},{9,8},{10,9},{11,1... | collective-permute-start | bytes 130568 | tf_op jit(solution)/shard_map/ppermute | solution.py:18
  15.6 0.3 collective-permute-done
  15.9 1.7 %copy.34 = f32[17,5,128]{1,0,2:T(8,128)} copy(f32[17,5,128]{2,0,1:T(8,128)S(1)} %collective-permute-done) | data formatting | bytes 87040 | tf_op jit(solution)/shard_map/ppermute | solution.py:17
  17.6 0.0 collective-permute-done.1
  17.6 1.7 %copy.35 = f32[17,5,128]{1,0,2:T(8,128)} copy(f32[17,5,128]{2,0,1:T(8,128)S(1)} %collective-permute-done.1) | data formatting | bytes 87040 | tf_op jit(solution)/shard_map/ppermute | solution.py:18
  19.2 1.1 %pad_maximum_fusion.6 = (f32[17,138,5]{1,0,2:T(8,128)S(1)}, f32[17,138,5]{1,0,2:T(8,128)S(1)}) fusion(f32[17,5,128]{1,0,2:T(8,128)} %copy.35, f32[17,5,128]{1,0,2:T(8,128)} %copy.34, f32[1,128,128]{1,0,2:T(1,128)S(1)} %bitcast.17, f32[16,128,128]{1,0,2:T(8,128)S(1)} %convert_multiply_fusion), kind=kLoop, calls=%fused_computation.70 | loop fusion | flops 70380 | bytes 1294992 | tf_op jit(solution)/shard_map/slice | solution.py:16
  20.3 1.3 %collective-permute-start.2 = (f32[17,138,5]{1,0,2:T(8,128)S(1)}, f32[17,138,5]{1,0,2:T(8,128)S(1)}, u32[]{:S(2)}, u32[]{:S(2)}) collective-permute-start(f32[17,138,5]{1,0,2:T(8,128)S(1)} %get-tuple-element.33), channel_id=1, source_target_pairs={{0,8},{8,16},{16,24},{1,9},{9,17},{17,25},{2,10},{10,18},{18,26},{... | collective-permute-start | bytes 140768 | tf_op jit(solution)/shard_map/ppermute | solution.py:17
  21.7 1.5 %collective-permute-start.3 = (f32[17,138,5]{1,0,2:T(8,128)S(1)}, f32[17,138,5]{1,0,2:T(8,128)S(1)}, u32[]{:S(2)}, u32[]{:S(2)}) collective-permute-start(f32[17,138,5]{1,0,2:T(8,128)S(1)} %get-tuple-element.34), channel_id=1, source_target_pairs={{8,0},{16,8},{24,16},{9,1},{17,9},{25,17},{10,2},{18,10},{26,18},{... | collective-permute-start | bytes 140768 | tf_op jit(solution)/shard_map/ppermute | solution.py:18
  23.1 0.0 copy-done.9
  23.1 0.1 copy.37
  23.2 0.0 collective-permute-done.2
  23.2 3.5 %collective-permute-done.3 = f32[17,138,5]{1,0,2:T(8,128)S(1)} collective-permute-done((f32[17,138,5]{1,0,2:T(8,128)S(1)}, f32[17,138,5]{1,0,2:T(8,128)S(1)}, u32[]{:S(2)}, u32[]{:S(2)}) %collective-permute-start.3) | collective-permute-done | bytes 46952 | tf_op jit(solution)/shard_map/ppermute | solution.py:18
  26.8 2.5 %fusion.22 = (f32[1,138,138]{1,0,2:T(1,128)S(1)}, f32[1,138,138]{1,0,2:T(1,128)S(1)}) fusion(f32[17,138,5]{1,0,2:T(8,128)S(1)} %collective-permute-done.3, f32[17,138,5]{1,0,2:T(8,128)S(1)} %collective-permute-done.2, f32[17,5,128]{1,0,2:T(8,128)} %copy.35, f32[17,5,128]{1,0,2:T(8,128)} %copy.34, f32[1,128,128]{1,0,2:T(1,128)S(1)} %bitcast.18, ...), kind=kLoop, calls=%fused_computation.63 | loop fusion | flops 266616 | bytes 1447344 | tf_op jit(solution)/shard_map/mul | solution.py:57
  29.3 0.0 copy-start.2
  29.3 0.1 slice.238
  29.5 0.1 slice.247
  29.6 0.1 slice.240
  29.7 0.1 slice.249
  29.8 0.1 slice.246
  29.9 0.1 slice.256
  30.0 0.1 slice.263
  30.1 0.1 slice.265
  30.2 0.1 slice.262
  30.3 0.1 slice.272
  30.4 0.3 copy-done.2
  30.7 1.3 %pad_maximum_fusion = f32[17,138,138]{1,0,2:T(8,128)S(1)} fusion(f32[17,138,5]{1,0,2:T(8,128)S(1)} %collective-permute-done.3, f32[17,5,128]{1,0,2:T(8,128)S(1)} %copy-done.3, f32[1,128,128]{1,0,2:T(1,128)S(1)} %bitcast.19, f32[16,128,128]{1,0,2:T(8,128)S(1)} %convert_multiply_fusion, f32[17,5,128]{1,0,2:T(8,128)S(1)} %copy-done.2, ...), kind=kLoop, calls=%fused_computation.2 | loop fusion | flops 1618740 | bytes 2589984 | tf_op jit(solution)/shard_map/concatenate | solution.py:19
  32.0 2.4 %fusion.7 = f32[16,136,136]{1,0,2:T(8,128)S(1)} fusion(f32[17,138,138]{1,0,2:T(8,128)S(1)} %pad_maximum_fusion, f32[136,136]{0,1:T(8,128)S(1)} %slice.240, f32[136,136]{0,1:T(8,128)S(1)} %slice.238), kind=kLoop, calls=%fused_computation.10 | loop fusion | flops 1775616 | bytes 7250432 | tf_op jit(solution)/shard_map/sub | solution.py:25
  34.4 0.0 copy-start
  34.4 2.9 %fusion.8 = f32[16,134,134]{1,0,2:T(8,128)S(1)} fusion(f32[17,138,138]{1,0,2:T(8,128)S(1)} %pad_maximum_fusion, f32[16,136,136]{1,0,2:T(8,128)S(1)} %fusion.7, f32[134,134]{0,1:T(8,128)S(1)} %slice.249, f32[134,134]{0,1:T(8,128)S(1)} %slice.247), kind=kLoop, calls=%fused_computation.15 | loop fusion | flops 2298368 | bytes 8187936 | tf_op jit(solution)/shard_map/sub | solution.py:65
  37.3 2.3 %fusion.12 = f32[16,132,132]{1,0,2:T(8,128)S(1)} fusion(f32[16,134,134]{1,0,2:T(8,128)S(1)} %fusion.8, f32[132,132]{0,1:T(8,128)S(1)} %slice.256, f32[132,132]{0,1:T(8,128)S(1)} %slice.246), kind=kLoop, calls=%fused_computation.24 | loop fusion | flops 1672704 | bytes 6830208 | tf_op jit(solution)/shard_map/sub | solution.py:25
  39.6 3.1 %fusion.13 = f32[16,130,130]{1,0,2:T(8,128)S(1)} fusion(f32[16,134,134]{1,0,2:T(8,128)S(1)} %fusion.8, f32[16,132,132]{1,0,2:T(8,128)S(1)} %fusion.12, f32[130,130]{0,1:T(8,128)S(1)} %slice.265, f32[130,130]{0,1:T(8,128)S(1)} %slice.263), kind=kLoop, calls=%fused_computation.29 | loop fusion | flops 2163200 | bytes 7706400 | tf_op jit(solution)/shard_map/sub | solution.py:67
  42.8 3.6 %multiply_reduce_fusion.6 = (f32[16]{0:T(128)S(1)}, f32[16]{0:T(128)S(1)}, f32[16]{0:T(128)S(1)}, f32[16]{0:T(128)S(1)}, f32[16]{0:T(128)S(1)}, /*index=5*/f32[1...) fusion(f32[16,136,136]{1,0,2:T(8,128)S(1)} %fusion.7, ...), kind=kLoop, calls=%fused_computation.56 | loop fusion | flops 8650608 | bytes 12845632 | tf_op jit(solution)/shard_map/reduce_sum | solution.py:72
  46.4 0.0 copy-done.1
  46.4 0.1 reshape.71
  46.5 3.3 %add_multiply_fusion = f32[16,128,128]{1,0,2:T(8,128)S(1)} fusion(f32[16,128,128]{1,0,2:T(8,128)} %get-tuple-element.26, f32[16,130,130]{1,0,2:T(8,128)} %copy-done.1, f32[16,136,136]{1,0,2:T(8,128)} %copy-done, f32[128,128]{0,1:T(8,128)S(1)} %copy.31, f32[128,128]{0,1:T(8,128)S(1)} %copy.30, s32[16,128,128]{1,0,2:T(8,128)S(1)} %copy.29), kind=kLoop, calls=%fused_computation.48 | loop fusion | flops 1572864 | bytes 5373952 | tf_op jit(solution)/shard_map/mul | solution.py:78
  49.8 0.0 copy-start.7
  49.8 1.0 copy-done.7
  50.8 0.0 copy-done.4
  50.8 2.4 %fusion.17 = f32[48,64]{1,0:T(8,128)S(1)} fusion(s32[128,128]{0,1:T(8,128)S(1)} %copy.37, f32[16,128,128]{1,0,2:T(8,128)S(1)} %add_multiply_fusion, f32[16,128,128]{1,0,2:T(8,128)S(1)} %copy-done.4, f32[16,128,128]{1,0,2:T(8,128)S(1)} %copy-done.5), kind=kOutput, calls=%fused_computation.39 | convolution fusion | flops 606601216 | bytes 3223552 | tf_op jit(solution)/shard_map/szt,zti->si/dot_general | solution.py:82
  53.2 0.1 reshape.72
  53.3 0.1 pad_maximum_fusion.7
  53.4 42.4 %psum.7 = f32[3216]{0:T(1024)S(1)} all-reduce(f32[3216]{0:T(1024)S(1)} %pad_maximum_fusion.7), channel_id=1, replica_groups=mesh['lat'=4,'lon'=8] {'lat','lon'}, use_global_device_ids=true, to_apply=%region_9.0 | all-reduce | flops 3216 | bytes 25728 | tf_op jit(solution)/shard_map/psum | solution.py:87
  95.8 0.1 fusion.30
  95.9 0.1 compare_select_fusion.2
  95.9 0.1 unstack.64
  96.0 0.1 unstack.66
  96.1 0.1 unstack.68
  96.1 0.1 multiply_subtract_fusion
  96.2 4.5 %multiply_add_fusion = (f32[16,128,128]{1,0,2:T(8,128)}, f32[16,128,128]{1,0,2:T(8,128)}) fusion(f32[16,128,128]{1,0,2:T(8,128)} %copy-done.7, f32[16,128,128]{1,0,2:T(8,128)} %get-tuple-element.29, f32[16,128,128]{1,0,2:T(8,128)} %get-tuple-element.35, f32[16]{0:T(128)S(1)} %get-tuple-element.23, f32[16]{0:T(128)S(1)} %get-tuple-element.22, ...), kind=kLoop, calls=%fused_computation.46 | loop fusion | flops 3145728 | bytes 8454336 | tf_op jit(solution)/shard_map/add | solution.py:93
  100.8 2.6 %copy.38 = f32[16,128,128]{2,1,0:T(8,128)} copy(f32[16,128,128]{1,0,2:T(8,128)} %get-tuple-element.42) | data formatting | bytes 2097152
  103.4 0.0 copy-done.6
  103.4 1.4 %copy.39 = f32[16,128,128]{2,1,0:T(8,128)} copy(f32[16,128,128]{1,0,2:T(8,128)S(1)} %copy-done.6) | data formatting | bytes 2097152
  104.8 0.7 add_multiply_fusion.2
  (11 shorter events, 0.1 us)
Async XLA Ops:
  0.6 2.7 %copy-start.8 = (f32[128,128]{1,0:T(8,128)S(1)}, f32[128,128]{1,0:T(8,128)}, u32[]{:S(2)}) copy-start(f32[128,128]{1,0:T(8,128)} %param.6) | copy-start | bytes 196612
  7.6 8.3 %collective-permute-start = (f32[17,5,128]{2,0,1:T(8,128)S(1)}, f32[17,5,128]{2,0,1:T(8,128)S(1)}, u32[]{:S(2)}, u32[]{:S(2)}) collective-permute-start(f32[17,5,128]{2,0,1:T(8,128)S(1)} %copy.32), channel_id=1, source_target_pairs={{0,1},{1,2},{2,3},{3,4},{4,5},{5,6},{6,7},{7,0},{8,9},{9,10},{10,1... | collective-permute-start | bytes 130568 | tf_op jit(solution)/shard_map/ppermute | solution.py:17
  12.5 5.1 %collective-permute-start.1 = (f32[17,5,128]{2,0,1:T(8,128)S(1)}, f32[17,5,128]{2,0,1:T(8,128)S(1)}, u32[]{:S(2)}, u32[]{:S(2)}) collective-permute-start(f32[17,5,128]{2,0,1:T(8,128)S(1)} %copy.33), channel_id=1, source_target_pairs={{1,0},{2,1},{3,2},{4,3},{5,4},{6,5},{7,6},{0,7},{9,8},{10,9},{11,1... | collective-permute-start | bytes 130568 | tf_op jit(solution)/shard_map/ppermute | solution.py:18
  19.2 3.9 %copy-start.9 = (s32[128,128]{1,0:T(8,128)S(1)}, s32[128,128]{1,0:T(8,128)}, u32[]{:S(2)}) copy-start(s32[128,128]{1,0:T(8,128)} %param.7) | copy-start | bytes 196612
  20.3 2.9 %collective-permute-start.2 = (f32[17,138,5]{1,0,2:T(8,128)S(1)}, f32[17,138,5]{1,0,2:T(8,128)S(1)}, u32[]{:S(2)}, u32[]{:S(2)}) collective-permute-start(f32[17,138,5]{1,0,2:T(8,128)S(1)} %get-tuple-element.33), channel_id=1, source_target_pairs={{0,8},{8,16},{16,24},{1,9},{9,17},{17,25},{2,10},{10,18},{18,26},{... | collective-permute-start | bytes 140768 | tf_op jit(solution)/shard_map/ppermute | solution.py:17
  21.7 5.1 %collective-permute-start.3 = (f32[17,138,5]{1,0,2:T(8,128)S(1)}, f32[17,138,5]{1,0,2:T(8,128)S(1)}, u32[]{:S(2)}, u32[]{:S(2)}) collective-permute-start(f32[17,138,5]{1,0,2:T(8,128)S(1)} %get-tuple-element.34), channel_id=1, source_target_pairs={{8,0},{16,8},{24,16},{9,1},{17,9},{25,17},{10,2},{18,10},{26,18},{... | collective-permute-start | bytes 140768 | tf_op jit(solution)/shard_map/ppermute | solution.py:18
  26.8 3.6 %copy-start.3 = (f32[17,5,128]{1,0,2:T(8,128)S(1)}, f32[17,5,128]{1,0,2:T(8,128)}, u32[]{:S(2)}) copy-start(f32[17,5,128]{1,0,2:T(8,128)} %copy.35) | copy-start | bytes 130564
  29.3 1.4 %copy-start.2 = (f32[17,5,128]{1,0,2:T(8,128)S(1)}, f32[17,5,128]{1,0,2:T(8,128)}, u32[]{:S(2)}) copy-start(f32[17,5,128]{1,0,2:T(8,128)} %copy.34) | copy-start | bytes 130564
  34.4 8.4 %copy-start = (f32[16,136,136]{1,0,2:T(8,128)}, f32[16,136,136]{1,0,2:T(8,128)S(1)}, u32[]{:S(2)}) copy-start(f32[16,136,136]{1,0,2:T(8,128)S(1)} %fusion.7) | copy-start | bytes 3551236
  42.8 3.6 %copy-start.1 = (f32[16,130,130]{1,0,2:T(8,128)}, f32[16,130,130]{1,0,2:T(8,128)S(1)}, u32[]{:S(2)}) copy-start(f32[16,130,130]{1,0,2:T(8,128)S(1)} %fusion.13) | copy-start | bytes 3244804
  46.5 4.3 %copy-start.4 = (f32[16,128,128]{1,0,2:T(8,128)S(1)}, f32[16,128,128]{1,0,2:T(8,128)}, u32[]{:S(2)}) copy-start(f32[16,128,128]{1,0,2:T(8,128)} %get-tuple-element.29) | copy-start | bytes 3145732
  46.5 4.3 %copy-start.5 = (f32[16,128,128]{1,0,2:T(8,128)S(1)}, f32[16,128,128]{1,0,2:T(8,128)}, u32[]{:S(2)}) copy-start(f32[16,128,128]{1,0,2:T(8,128)} %get-tuple-element.35) | copy-start | bytes 3145732
  49.8 1.0 copy-start.7
  100.8 2.6 %copy-start.6 = (f32[16,128,128]{1,0,2:T(8,128)S(1)}, f32[16,128,128]{1,0,2:T(8,128)}, u32[]{:S(2)}) copy-start(f32[16,128,128]{1,0,2:T(8,128)} %get-tuple-element.41) | copy-start | bytes 3145732
where the time goes:
time: 106 us; the launch traced here: 105 us
  blocking collectives  42.4 us (40%)
  other arithmetic  31.1 us (29%)
  local copies, waits for them, and re-layouts  15.9 us (15%)
  starting transfers between devices  8.85 us (8%)
  waiting for transfers between devices  3.85 us (4%)
  matrix products  2.44 us (2%)
    psum x1, blocking collectives, per_device(): both = lax.psum(both, ('lat', 'lon'))  42.4 us
    unnamed x26, local copies, waits for them, and re-layouts  7.31 us
    sub x2, other arithmetic, stencil(): return centre * field[:, 1:-1, 1:-1] - side * total  4.65 us
    ppermute x2, starting transfers between devices, extended(): lax.ppermute(head, axis, [((i + 1) % count, i) for i in range(ends)])  4.56 us
    add x1, other arithmetic, per_device(): trace = yf[0] * terms[0] + yf[1] * terms[1] + yf[2] * terms[2]  4.55 us
    ppermute x2, starting transfers between devices, extended(): lax.ppermute(tail, axis, [(i, (i + 1) % count) for i in range(ends)])  4.29 us
    reduce_sum x1, other arithmetic, dot(): return jnp.sum(a * b, axis=(1, 2))  3.59 us
    ppermute x2, waiting for transfers between devices, extended(): lax.ppermute(head, axis, [((i + 1) % count, i) for i in range(ends)])  3.51 us
  transfers between devices with their start and end apart: 4, of which 2 were waited for; matrix products, arithmetic and copies ran while one was open for 3% of the time, Pallas kernels for 0%

commit v1 on v0

v1 whole, which is shorter than its diff:
```python
import functools

import jax
import jax.numpy as jnp
from jax import lax
from jax.experimental import pallas as pl
from jax.experimental.pallas import tpu as pltpu
from jax.sharding import PartitionSpec as P

NB = 64
EDGE = 7
PAD = 8
SHIFT = 0.4
FLOOR = 1e-6
CHUNK = 48
MESH = pl.DeviceIdType.MESH


def weights(gram, right):
    g00, g01, g02, g11, g12, g22 = gram
    r0, r1, r2 = right
    l10 = g01 / g00
    l20 = g02 / g00
    d1 = g11 - l10 * g01
    e12 = g12 - l10 * g02
    ok1 = d1 > FLOOR * g11
    i1 = jnp.where(ok1, 1.0 / jnp.where(ok1, d1, 1.0), 0.0)
    l21 = e12 * i1
    d2 = g22 - l20 * g02 - l21 * e12
    ok2 = d2 > FLOOR * g22
    i2 = jnp.where(ok2, 1.0 / jnp.where(ok2, d2, 1.0), 0.0)
    z1 = r1 - l10 * r0
    z2 = r2 - l20 * r0 - l21 * z1
    y2 = z2 * i2
    y1 = z1 * i1 - l21 * y2
    y0 = r0 / g00 - l10 * y1 - l20 * y2
    return y0, y1, y2


def kernel(
    nlat, nlon, signs, mask, kappa, ids, solved, trace, traces,
    planes, halo, left_edge, right_edge, coef, work, kept, terms, dots, ys,
    gram_lat, gram_lon, sums_lat, sums_lon,
    halo_send, halo_recv, lat_send, lat_recv, lon_send, lon_recv,
):
    count, rows, lanes = signs.shape
    ext = rows + 2 * PAD
    lat, lon = lax.axis_index("lat"), lax.axis_index("lon")
    up, down = lax.rem(lon + 1, nlon), lax.rem(lon + nlon - 1, nlon)

    barrier = pltpu.get_barrier_semaphore()
    for d in range(1, nlat):
        pl.semaphore_signal(
            barrier, inc=1, device_id=(lax.rem(lat + d, nlat), lon), device_id_type=MESH)
    for d in range(1, nlon):
        pl.semaphore_signal(
            barrier, inc=1, device_id=(lat, lax.rem(lon + d, nlon)), device_id_type=MESH)

    lane = lax.broadcasted_iota(jnp.int32, (1, lanes), 1)

    def pack(step, carry):
        part = pl.ds(pl.multiple_of(step * 32, 32), 32)
        ocean = mask[part, :].astype(jnp.float32)
        first = jnp.zeros((32, lanes), jnp.float32)
        last = jnp.zeros((32, lanes), jnp.float32)
        for p in range(count + 1):
            if p < count:
                x = signs[p, part, :].astype(jnp.float32) * ocean
            else:
                x = kappa[part, :]
            planes[p, pl.ds(pl.multiple_of(step * 32 + PAD, 8), 32), :] = x
            here = (lane >= EDGE * p) & (lane < EDGE * (p + 1))
            first = jnp.where(here, pltpu.roll(x, EDGE * p, 1) if p else x, first)
            last = jnp.where(here, pltpu.roll(x, EDGE * (p + 1), 1), last)
        left_edge[part, :] = first
        right_edge[part, :] = last
        return carry

    lax.fori_loop(0, rows // 32, pack, 0)
    pl.semaphore_wait(barrier, nlat + nlon - 2)

    def copy(src, dst, k, device):
        return pltpu.make_async_remote_copy(
            src_ref=src, dst_ref=dst, send_sem=halo_send.at[k], recv_sem=halo_recv.at[k],
            device_id=device, device_id_type=MESH)

    own = pl.ds(PAD, rows)
    top, low = pl.ds(rows, PAD), pl.ds(PAD, PAD)
    before, after = pl.ds(0, PAD), pl.ds(rows + PAD, PAD)
    go_right = copy(right_edge, halo.at[0, own, :], 0, (lax.min(lat + 1, nlat - 1), lon))
    go_left = copy(left_edge, halo.at[1, own, :], 1, (lax.max(lat - 1, 0), lon))
    go_up = copy(planes.at[:, top, :], planes.at[:, before, :], 2, (lat, up))
    go_down = copy(planes.at[:, low, :], planes.at[:, after, :], 3, (lat, down))
    halo_up = copy(halo.at[:, top, :], halo.at[:, before, :], 4, (lat, up))
    halo_down = copy(halo.at[:, low, :], halo.at[:, after, :], 5, (lat, down))

    @pl.when(lat < nlat - 1)
    def _():
        go_right.start()

    @pl.when(lat > 0)
    def _():
        go_left.start()

    go_up.start()
    go_down.start()

    @pl.when(lat == 0)
    def _():
        halo[0, PAD:PAD + rows, :] = jnp.zeros((rows, lanes), jnp.float32)

    @pl.when(lat == nlat - 1)
    def _():
        halo[1, PAD:PAD + rows, :] = jnp.zeros((rows, lanes), jnp.float32)

    for k in range(work.shape[0]):
        for s in range(2):
            work[k, s, 0:PAD, :] = jnp.zeros((PAD, lanes), jnp.float32)
            work[k, s, ext + PAD:ext + 2 * PAD, :] = jnp.zeros((PAD, lanes), jnp.float32)

    @pl.when(lat > 0)
    def _():
        go_right.wait_recv()

    @pl.when(lat < nlat - 1)
    def _():
        go_left.wait_recv()

    halo_up.start()
    halo_down.start()
    go_up.wait()
    go_down.wait()
    halo_up.wait()
    halo_down.wait()

    @pl.when(lat < nlat - 1)
    def _():
        go_right.wait_send()

    @pl.when(lat > 0)
    def _():
        go_left.wait_send()

    chunks = [(a, min(CHUNK, ext - a)) for a in range(0, ext, CHUNK)]

    def unpack(p, a, n):
        left = pltpu.roll(halo[0, a:a + n, :], lax.rem(2 * lanes - EDGE - EDGE * p, lanes), 1)
        right = pltpu.roll(halo[1, a:a + n, :], lax.rem(2 * lanes - EDGE * p, lanes), 1)
        return jnp.where(lane < EDGE, right, jnp.where(lane >= lanes - EDGE, left, 0.0))

    for a, n in chunks:
        for s in range(2):
            if s:
                ocean, k = unpack(0, a, n), unpack(count, a, n)
            else:
                ocean, k = planes[0, a:a + n, :], planes[count, a:a + n, :]
            ocean = ocean * ocean
            coef[0, s, a:a + n, :] = ocean * (k + 0.25)
            coef[1, s, a:a + n, :] = 0.0625 * ocean

    at_first, at_last = lane == 0, lane == lanes - 1

    def apply(src, a, n, wide):
        o = a + PAD
        m, h = work[src, 0, o:o + n, :], work[src, 1, o:o + n, :]
        m_right, h_right = pltpu.roll(m, 1, 1), pltpu.roll(h, 1, 1)
        m_left, h_left = pltpu.roll(m, lanes - 1, 1), pltpu.roll(h, lanes - 1, 1)

        def one(s, x, a_side, b_side):
            total = work[src, s, o - 1:o + n - 1, :] + work[src, s, o + 1:o + n + 1, :]
            total = total + a_side + b_side
            return coef[0, s, a:a + n, :] * x - coef[1, s, a:a + n, :] * total

        out = one(0, m, jnp.where(at_first, h_right, m_right), jnp.where(at_last, h_left, m_left))
        if not wide:
            return out, None
        return out, one(
            1, h, jnp.where(at_first, m_right, h_right), jnp.where(at_last, m_left, h_left))

    def put(dst, a, n, pair):
        o = a + PAD
        work[dst, 0, o:o + n, :] = pair[0]
        work[dst, 1, o:o + n, :] = pair[1]

    def get(src, a, n):
        o = a + PAD
        return work[src, 0, o:o + n, :], work[src, 1, o:o + n, :]

    def probe(p, carry):
        for a, n in chunks:
            put(0, a, n, (planes[p, a:a + n, :], unpack(p, a, n)))
        for k in range(3):
            for a, n in chunks:
                put(k + 1, a, n, apply(k, a, n, True))
        for a, n in chunks:
            m, h = apply(3, a, n, True)
            m_old, h_old = get(2, a, n)
            put(4, a, n, (m - SHIFT * m_old, h - SHIFT * h_old))
        part = [jnp.zeros((8, lanes), jnp.float32) for _ in range(7)]
        step = 32
        for a in range(0, rows, step):
            w2, _ = apply(4, a + PAD, step, False)
            v0, w0, v1, w1, v2 = (get(k, a + PAD, step)[0] for k in range(5))
            k = kappa[a:a + step, :]
            kept[0, p, a:a + step, :] = v1
            kept[1, p, a:a + step, :] = v2
            for j, (v, w) in enumerate(((v0, w0), (v1, w1), (v2, w2))):
                at = pl.ds(pl.multiple_of((j * count + p) * rows + a, 8), step)
                terms[at, :] = k * (2.0 * v0 * w0) if j == 0 else k * (v * w0 + w * v0)
            pairs = ((w0, w0), (w0, w1), (w0, w2), (w1, w1), (w1, w2), (w2, w2), (v0, v0))
            for j, (x, y) in enumerate(pairs):
                xy = x * y
                for i in range(0, step, 8):
                    part[j] = part[j] + xy[i:i + 8]
        for j in range(7):
            dots[j, pl.ds(p, 1), :] = jnp.sum(part[j], axis=0, keepdims=True)
        return carry

    lax.fori_loop(0, count, probe, 0)

    def share(buf, mine, n, send, recv, axis):
        copies = []
        for d in range(1, n):
            other = lax.rem(mine + d, n)
            source = lax.rem(mine + n - d, n)
            device = (other, lon) if axis == 0 else (lat, other)
            pltpu.make_async_remote_copy(
                src_ref=buf.at[mine], dst_ref=buf.at[mine],
                send_sem=send.at[d - 1], recv_sem=recv.at[d - 1],
                device_id=device, device_id_type=MESH).start()
            copies.append(pltpu.make_async_remote_copy(
                src_ref=buf.at[mine], dst_ref=buf.at[source],
                send_sem=send.at[d - 1], recv_sem=recv.at[d - 1],
                device_id=device, device_id_type=MESH))
        return copies

    def gather(buf, n, copies):
        for c in copies:
            c.wait()
        total = buf[0]
        for i in range(1, n):
            total = total + buf[i]
        return total

    mine = jnp.zeros((count, lanes), jnp.float32)
    for j in range(7):
        mine = jnp.where(lane == j, jnp.sum(dots[j], axis=1, keepdims=True), mine)
    gram_lat[lat] = mine
    sent = share(gram_lat, lat, nlat, lat_send.at[0], lat_recv.at[0], 0)

    block = lax.broadcasted_iota(jnp.int32, (NB, lanes), 0)

    def sums(step, acc):
        lhs, rhs = [], []
        for i in range(2):
            z = step * 2 + i
            x = terms[pl.ds(z, 3 * count, stride=rows), :]
            high = x.astype(jnp.bfloat16)
            low = (x - high.astype(jnp.float32)).astype(jnp.bfloat16)
            lhs.append(jnp.concatenate([high, low], axis=0))
            hit = jnp.where(ids[pl.ds(z, 1), :] == block, 1.0, 0.0)
            rhs.append(hit.astype(jnp.bfloat16))
        return acc + lax.dot_general(
            jnp.concatenate(lhs, axis=1), jnp.concatenate(rhs, axis=1),
            (((1,), (1,)), ((), ())), preferred_element_type=jnp.float32)

    acc = jnp.zeros((6 * count, NB), jnp.float32)
    acc = lax.fori_loop(0, rows // 4, sums, acc, unroll=4)
    gram_lon[lon] = gather(gram_lat, nlat, sent)
    sent = share(gram_lon, lon, nlon, lon_send.at[0], lon_recv.at[0], 1)
    acc = lax.fori_loop(rows // 4, rows // 2, sums, acc, unroll=4)
    total = gather(gram_lon, nlon, sent)

    g = [total[:, j:j + 1] for j in range(7)]
    y = weights(tuple(g[:6]), (g[6], g[0], g[1] - SHIFT * g[0]))
    local = jnp.zeros((count, NB), jnp.float32)
    for j in range(3):
        ys[j] = jnp.broadcast_to(y[j], (count, lanes))
        at = j * count
        local = local + y[j] * (acc[at:at + count] + acc[at + 3 * count:at + 4 * count])
    sums_lat[lat] = jnp.concatenate([local, jnp.zeros_like(local)], axis=1)
    sent = share(sums_lat, lat, nlat, lat_send.at[1], lat_recv.at[1], 0)

    def finish(p, carry):
        y0, y1, y2 = (ys[j, pl.ds(p, 1), :] for j in range(3))
        solved[p] = y0 * planes[p, PAD:PAD + rows, :] + y1 * kept[0, p] + y2 * kept[1, p]
        t = [
            terms[pl.ds(pl.multiple_of((j * count + p) * rows, 8), rows), :] for j in range(3)]
        trace[p] = y0 * t[0] + y1 * t[1] + y2 * t[2]
        return carry

    lax.fori_loop(0, count // 2, finish, 0)
    sums_lon[lon] = gather(sums_lat, nlat, sent)
    sent = share(sums_lon, lon, nlon, lon_send.at[1], lon_recv.at[1], 1)
    lax.fori_loop(count // 2, count, finish, 0)
    total = gather(sums_lon, nlon, sent)
    traces[...] = total[:, :NB] * (NB / (rows * lanes * nlat * nlon))


def per_device(nlat, nlon, probe_signs, ocean_mask, kappa_sq, block_ids):
    count, rows, lanes = probe_signs.shape
    ext = rows + 2 * PAD
    f32 = jnp.float32
    vmem = pl.BlockSpec(memory_space=pltpu.VMEM)
    return pl.pallas_call(
        functools.partial(kernel, nlat, nlon),
        out_shape=(
            jax.ShapeDtypeStruct((count, rows, lanes), f32),
            jax.ShapeDtypeStruct((count, rows, lanes), f32),
            jax.ShapeDtypeStruct((count, NB), f32),
        ),
        in_specs=[vmem] * 4,
        out_specs=(vmem,) * 3,
        scratch_shapes=[
            pltpu.VMEM((count + 1, ext, lanes), f32),
            pltpu.VMEM((2, ext, lanes), f32),
            pltpu.VMEM((rows, lanes), f32),
            pltpu.VMEM((rows, lanes), f32),
            pltpu.VMEM((2, 2, ext, lanes), f32),
            pltpu.VMEM((5, 2, ext + 2 * PAD, lanes), f32),
            pltpu.VMEM((2, count, rows, lanes), f32),
            pltpu.VMEM((3 * count * rows, lanes), f32),
            pltpu.VMEM((8, count, lanes), f32),
            pltpu.VMEM((3, count, lanes), f32),
            pltpu.VMEM((nlat, count, lanes), f32),
            pltpu.VMEM((nlon, count, lanes), f32),
            pltpu.VMEM((nlat, count, lanes), f32),
            pltpu.VMEM((nlon, count, lanes), f32),
            pltpu.SemaphoreType.DMA((6,)),
            pltpu.SemaphoreType.DMA((6,)),
            pltpu.SemaphoreType.DMA((2, nlat - 1)),
            pltpu.SemaphoreType.DMA((2, nlat - 1)),
            pltpu.SemaphoreType.DMA((2, nlon - 1)),
            pltpu.SemaphoreType.DMA((2, nlon - 1)),
        ],
        compiler_params=pltpu.CompilerParams(
            collective_id=0, has_side_effects=True, vmem_limit_bytes=40 * 1024 * 1024),
    )(probe_signs, ocean_mask, kappa_sq, block_ids)


def solution(mesh):
    placed = (P(None, "lon", "lat"), P("lon", "lat"), P("lon", "lat"), P("lon", "lat"))
    return jax.shard_map(
        functools.partial(per_device, mesh.shape["lat"], mesh.shape["lon"]),
        mesh=mesh,
        in_specs=placed,
        out_specs=(P(None, "lon", "lat"), P(None, "lon", "lat"), P()),
        check_vma=False,
    )
```

time: 106 us -> 43.4 us (0.41)
  blocking collectives: 42.4 us -> 0 us
  Pallas kernels: 0 us -> 36.2 us
  other arithmetic: 31.1 us -> 0 us
  local copies, waits for them, and re-layouts: 15.9 us -> 6.27 us
  starting transfers between devices: 8.85 us -> 0 us
  waiting for transfers between devices: 3.85 us -> 0 us
  matrix products: 2.44 us -> 0 us
    psum x1 -> x0, blocking collectives: 42.4 us -> none  [per_device(): both = lax.psum(both, ('lat', 'lon'))]
    pallas_call x0 -> x1, Pallas kernels: none -> 36.2 us  [per_device(): pl.pallas_call(functools.partial(kernel, nlat, nlon), out_shape=(jax.Shap...]
    sub x5 -> x0, other arithmetic: 10.8 us -> none  [the longest x2 4.65 us: stencil(): return centre * field[:, 1:-1, 1:-1] - side * total]
    ppermute x4 -> x0, starting transfers between devices: 8.85 us -> none  [the longest x2 4.56 us: extended(): lax.ppermute(head, axis, [((i + 1) % count, i) for i in range(ends)])]
    mul x3 -> x0, other arithmetic: 5.94 us -> none  [the longest x1 3.3 us: per_device(): kappa_sq * (v * w0 + w * v0)]
    slice x12 -> x0, local copies, waits for them, and re-layouts: 4.73 us -> none  [the longest x1 1.88 us: extended(): lax.slice_in_dim(cells, cells.shape[dim] - width, cells.shape[dim], axis=...]
    add x1 -> x0, other arithmetic: 4.55 us -> none  [per_device(): trace = yf[0] * terms[0] + yf[1] * terms[1] + yf[2] * terms[2]]
    ppermute x4 -> x0, waiting for transfers between devices: 3.85 us -> none  [the longest x2 3.51 us: extended(): lax.ppermute(head, axis, [((i + 1) % count, i) for i in range(ends)])]
  transfers between devices with their start and end apart: 4 -> 0, of which waited for: 2 -> 0; matrix products, arithmetic and copies ran while one was open for 3% -> 0% of each run, Pallas kernels for 0% -> 0%
where the time goes in v1:
time: 43.4 us; the launch traced here: 43.2 us
  Pallas kernels  36.2 us (83%)
  local copies, waits for them, and re-layouts  6.27 us (14%)
  between operations  0.65 us (1%)
    pallas_call x1, Pallas kernels, per_device(): pl.pallas_call(functools.partial(kernel, nlat, nlon), out_shape=(jax.Shap...  36.2 us
    unnamed x11, local copies, waits for them, and re-layouts  6.27 us

profile of v1, /device:TPU:0, one launch (start us, length us, event | category | flops | bytes accessed | tf_op | source)
XLA Modules:
  0.0 43.2 jit_solution(13430627612094787558)
XLA Ops:
  0.6 0.0 copy-start
  0.6 1.2 %copy-done = s32[16,128,128]{2,1,0:T(8,128)S(1)} copy-done((s32[16,128,128]{2,1,0:T(8,128)S(1)}, s32[16,128,128]{2,1,0:T(8,128)}, u32[]{:S(2)}) %copy-start) | copy-done | bytes 1048600
  1.9 0.0 copy-start.1
  1.9 0.8 %copy-done.1 = s32[128,128]{1,0:T(8,128)S(1)} copy-done((s32[128,128]{1,0:T(8,128)S(1)}, s32[128,128]{1,0:T(8,128)}, u32[]{:S(2)}) %copy-start.1) | copy-done | bytes 65560
  2.7 0.0 copy-start.2
  2.7 0.8 %copy-done.2 = f32[128,128]{1,0:T(8,128)S(1)} copy-done((f32[128,128]{1,0:T(8,128)S(1)}, f32[128,128]{1,0:T(8,128)}, u32[]{:S(2)}) %copy-start.2) | copy-done | bytes 65560
  3.5 0.0 copy-start.3
  3.5 0.8 %copy-done.3 = s32[128,128]{1,0:T(8,128)S(1)} copy-done((s32[128,128]{1,0:T(8,128)S(1)}, s32[128,128]{1,0:T(8,128)}, u32[]{:S(2)}) %copy-start.3) | copy-done | bytes 65560
  4.4 36.2 %shard_map.67 = (f32[16,128,128]{2,1,0:T(8,128)S(1)}, f32[16,128,128]{2,1,0:T(8,128)S(1)}, f32[16,64]{1,0:T(8,128)S(1)}) custom-call(s32[16,128,128]{2,1,0:T(8,128)S(1)} %copy-done, s32[128,128]{1,0:T(8,128)S(1)} %copy-done.1, f32[128,128]{1,0:T(8,128)S(1)} %copy-done.2, s32[128,128]{1,0:T(8,128)S(1)} %copy-done.3), custom_call_target="tpu_custom_call" | custom-call | tf_op jit(solution)/shard_map/pallas_call | solution.py:305
  40.6 1.0 %copy.10 = f32[16,128,128]{2,1,0:T(8,128)} copy(f32[16,128,128]{2,1,0:T(8,128)S(1)} %get-tuple-element.6) | data formatting | bytes 2097152
  41.6 1.0 %copy.11 = f32[16,128,128]{2,1,0:T(8,128)} copy(f32[16,128,128]{2,1,0:T(8,128)S(1)} %get-tuple-element.7) | data formatting | bytes 2097152
  42.6 0.6 %copy.12 = f32[16,64]{1,0:T(8,128)} copy(f32[16,64]{1,0:T(8,128)S(1)} %get-tuple-element.8) | data formatting | bytes 8192
Async XLA Ops:
  0.6 1.2 %copy-start = (s32[16,128,128]{2,1,0:T(8,128)S(1)}, s32[16,128,128]{2,1,0:T(8,128)}, u32[]{:S(2)}) copy-start(s32[16,128,128]{2,1,0:T(8,128)} %signs.1) | copy-start | bytes 3145732
  1.9 0.8 %copy-start.1 = (s32[128,128]{1,0:T(8,128)S(1)}, s32[128,128]{1,0:T(8,128)}, u32[]{:S(2)}) copy-start(s32[128,128]{1,0:T(8,128)} %mask.1) | copy-start | bytes 196612
  2.7 0.8 %copy-start.2 = (f32[128,128]{1,0:T(8,128)S(1)}, f32[128,128]{1,0:T(8,128)}, u32[]{:S(2)}) copy-start(f32[128,128]{1,0:T(8,128)} %kappa.1) | copy-start | bytes 196612
  3.5 0.8 %copy-start.3 = (s32[128,128]{1,0:T(8,128)S(1)}, s32[128,128]{1,0:T(8,128)}, u32[]{:S(2)}) copy-start(s32[128,128]{1,0:T(8,128)} %ids.1) | copy-start | bytes 196612

commit v2 on v1

--- a/solution.py
+++ b/solution.py
@@ -38,11 +38,18 @@
 
 
 def kernel(
-    nlat, nlon, signs, mask, kappa, ids, solved, trace, traces,
-    planes, halo, left_edge, right_edge, coef, work, kept, terms, dots, ys,
+    nlat, nlon, signs_in, mask_in, kappa_in, ids_in, solved, trace, traces,
+    signs, mask, kappa, ids, hits, planes, halo, left_edge, right_edge, coef, work, kept, terms, dots, ys,
     gram_lat, gram_lon, sums_lat, sums_lon,
-    halo_send, halo_recv, lat_send, lat_recv, lon_send, lon_recv,
+    load_done, halo_send, halo_recv, lat_send, lat_recv, lon_send, lon_recv,
 ):
+    loads = [
+        pltpu.make_async_copy(src, dst, load_done.at[k])
+        for k, (src, dst) in enumerate(
+            ((signs_in, signs), (mask_in, mask), (kappa_in, kappa), (ids_in, ids)))]
+    for load in loads:
+        load.start()
+
     count, rows, lanes = signs.shape
     ext = rows + 2 * PAD
     lat, lon = lax.axis_index("lat"), lax.axis_index("lon")
@@ -55,7 +62,17 @@
     for d in range(1, nlon):
         pl.semaphore_signal(
             barrier, inc=1, device_id=(lat, lax.rem(lon + d, nlon)), device_id_type=MESH)
-
+    has_left, has_right = lat > 0, lat < nlat - 1
+    left, right = lax.max(lat - 1, 0), lax.min(lat + 1, nlat - 1)
+    for there, side in ((has_left, left), (has_right, right)):
+        @pl.when(there)
+        def _(side=side):
+            for end in (up, down):
+                pl.semaphore_signal(
+                    barrier, inc=1, device_id=(side, end), device_id_type=MESH)
+
+    for load in loads[:3]:
+        load.wait()
     lane = lax.broadcasted_iota(jnp.int32, (1, lanes), 1)
 
     def pack(step, carry):
@@ -77,7 +94,8 @@
         return carry
 
     lax.fori_loop(0, rows // 32, pack, 0)
-    pl.semaphore_wait(barrier, nlat + nlon - 2)
+    sides = lax.min(lat, 1) + lax.min(nlat - 1 - lat, 1)
+    pl.semaphore_wait(barrier, nlat + nlon - 2 + 2 * sides)
 
     def copy(src, dst, k, device):
         return pltpu.make_async_remote_copy(
@@ -87,59 +105,74 @@
     own = pl.ds(PAD, rows)
     top, low = pl.ds(rows, PAD), pl.ds(PAD, PAD)
     before, after = pl.ds(0, PAD), pl.ds(rows + PAD, PAD)
-    go_right = copy(right_edge, halo.at[0, own, :], 0, (lax.min(lat + 1, nlat - 1), lon))
-    go_left = copy(left_edge, halo.at[1, own, :], 1, (lax.max(lat - 1, 0), lon))
-    go_up = copy(planes.at[:, top, :], planes.at[:, before, :], 2, (lat, up))
-    go_down = copy(planes.at[:, low, :], planes.at[:, after, :], 3, (lat, down))
-    halo_up = copy(halo.at[:, top, :], halo.at[:, before, :], 4, (lat, up))
-    halo_down = copy(halo.at[:, low, :], halo.at[:, after, :], 5, (lat, down))
-
-    @pl.when(lat < nlat - 1)
-    def _():
-        go_right.start()
-
-    @pl.when(lat > 0)
-    def _():
-        go_left.start()
-
-    go_up.start()
-    go_down.start()
+    first_rows, last_rows = pl.ds(0, PAD), pl.ds(rows - PAD, PAD)
+    go_right = [
+        copy(right_edge, halo.at[0, own, :], 0, (right, lon)),
+        copy(right_edge.at[last_rows, :], halo.at[0, before, :], 1, (right, up)),
+        copy(right_edge.at[first_rows, :], halo.at[0, after, :], 2, (right, down)),
+    ]
+    go_left = [
+        copy(left_edge, halo.at[1, own, :], 3, (left, lon)),
+        copy(left_edge.at[last_rows, :], halo.at[1, before, :], 4, (left, up)),
+        copy(left_edge.at[first_rows, :], halo.at[1, after, :], 5, (left, down)),
+    ]
+    go_lon = [
+        copy(planes.at[:, top, :], planes.at[:, before, :], 6, (lat, up)),
+        copy(planes.at[:, low, :], planes.at[:, after, :], 7, (lat, down)),
+    ]
+
+    @pl.when(has_right)
+    def _():
+        for c in go_right:
+            c.start()
+
+    @pl.when(has_left)
+    def _():
+        for c in go_left:
+            c.start()
+
+    for c in go_lon:
+        c.start()
 
     @pl.when(lat == 0)
     def _():
-        halo[0, PAD:PAD + rows, :] = jnp.zeros((rows, lanes), jnp.float32)
+        halo[0] = jnp.zeros((ext, lanes), jnp.float32)
 
     @pl.when(lat == nlat - 1)
     def _():
-        halo[1, PAD:PAD + rows, :] = jnp.zeros((rows, lanes), jnp.float32)
+        halo[1] = jnp.zeros((ext, lanes), jnp.float32)
 
     for k in range(work.shape[0]):
         for s in range(2):
             work[k, s, 0:PAD, :] = jnp.zeros((PAD, lanes), jnp.float32)
             work[k, s, ext + PAD:ext + 2 * PAD, :] = jnp.zeros((PAD, lanes), jnp.float32)
 
-    @pl.when(lat > 0)
-    def _():
-        go_right.wait_recv()
-
-    @pl.when(lat < nlat - 1)
-    def _():
-        go_left.wait_recv()
-
-    halo_up.start()
-    halo_down.start()
-    go_up.wait()
-    go_down.wait()
-    halo_up.wait()
-    halo_down.wait()
-
-    @pl.when(lat < nlat - 1)
-    def _():
-        go_right.wait_send()
-
-    @pl.when(lat > 0)
-    def _():
-        go_left.wait_send()
+    loads[3].wait()
+    block = lax.broadcasted_iota(jnp.int32, (NB, lanes), 0)
+
+    def mark(z, carry):
+        hit = jnp.where(ids[pl.ds(z, 1), :] == block, 1.0, 0.0)
+        hits[pl.ds(pl.multiple_of(z * NB, NB), NB), :] = hit.astype(jnp.bfloat16)
+        return carry
+
+    lax.fori_loop(0, rows, mark, 0, unroll=4)
+
+    for c in go_lon:
+        c.wait()
+
+    @pl.when(has_left)
+    def _():
+        for c in go_right:
+            c.wait_recv()
+        for c in go_left:
+            c.wait_send()
+
+    @pl.when(has_right)
+    def _():
+        for c in go_left:
+            c.wait_recv()
+        for c in go_right:
+            c.wait_send()
 
     chunks = [(a, min(CHUNK, ext - a)) for a in range(0, ext, CHUNK)]
 
@@ -248,8 +281,6 @@
     gram_lat[lat] = mine
     sent = share(gram_lat, lat, nlat, lat_send.at[0], lat_recv.at[0], 0)
 
-    block = lax.broadcasted_iota(jnp.int32, (NB, lanes), 0)
-
     def sums(step, acc):
         lhs, rhs = [], []
         for i in range(2):
@@ -258,8 +289,7 @@
             high = x.astype(jnp.bfloat16)
             low = (x - high.astype(jnp.float32)).astype(jnp.bfloat16)
             lhs.append(jnp.concatenate([high, low], axis=0))
-            hit = jnp.where(ids[pl.ds(z, 1), :] == block, 1.0, 0.0)
-            rhs.append(hit.astype(jnp.bfloat16))
+            rhs.append(hits[pl.ds(pl.multiple_of(z * NB, NB), NB), :])
         return acc + lax.dot_general(
             jnp.concatenate(lhs, axis=1), jnp.concatenate(rhs, axis=1),
             (((1,), (1,)), ((), ())), preferred_element_type=jnp.float32)
@@ -269,17 +299,21 @@
     gram_lon[lon] = gather(gram_lat, nlat, sent)
     sent = share(gram_lon, lon, nlon, lon_send.at[0], lon_recv.at[0], 1)
     acc = lax.fori_loop(rows // 4, rows // 2, sums, acc, unroll=4)
+    half = 3 * count // 2
+    acc = acc[:3 * count] + acc[3 * count:]
+    sums_lat[lat] = jnp.concatenate([acc[:half], acc[half:]], axis=1)
+    sums_sent = share(sums_lat, lat, nlat, lat_send.at[1], lat_recv.at[1], 0)
     total = gather(gram_lon, nlon, sent)
 
     g = [total[:, j:j + 1] for j in range(7)]
     y = weights(tuple(g[:6]), (g[6], g[0], g[1] - SHIFT * g[0]))
-    local = jnp.zeros((count, NB), jnp.float32)
     for j in range(3):
         ys[j] = jnp.broadcast_to(y[j], (count, lanes))
-        at = j * count
-        local = local + y[j] * (acc[at:at + count] + acc[at + 3 * count:at + 4 * count])
-    sums_lat[lat] = jnp.concatenate([local, jnp.zeros_like(local)], axis=1)
-    sent = share(sums_lat, lat, nlat, lat_send.at[1], lat_recv.at[1], 0)
+    acc = gather(sums_lat, nlat, sums_sent)
+    acc = jnp.concatenate([acc[:, :NB], acc[:, NB:]], axis=0)
+    local = y[0] * acc[:count] + y[1] * acc[count:2 * count] + y[2] * acc[2 * count:]
+    sums_lon[lon] = jnp.concatenate([local[:count // 2], local[count // 2:]], axis=1)
+    sent = share(sums_lon, lon, nlon, lon_send.at[1], lon_recv.at[1], 1)
 
     def finish(p, carry):
         y0, y1, y2 = (ys[j, pl.ds(p, 1), :] for j in range(3))
@@ -289,12 +323,10 @@
         trace[p] = y0 * t[0] + y1 * t[1] + y2 * t[2]
         return carry
 
-    lax.fori_loop(0, count // 2, finish, 0)
-    sums_lon[lon] = gather(sums_lat, nlat, sent)
-    sent = share(sums_lon, lon, nlon, lon_send.at[1], lon_recv.at[1], 1)
-    lax.fori_loop(count // 2, count, finish, 0)
+    lax.fori_loop(0, count, finish, 0)
     total = gather(sums_lon, nlon, sent)
-    traces[...] = total[:, :NB] * (NB / (rows * lanes * nlat * nlon))
+    total = jnp.concatenate([total[:, :NB], total[:, NB:]], axis=0)
+    traces[...] = total / jnp.float32(rows * lanes * nlat * nlon // NB)
 
 
 def per_device(nlat, nlon, probe_signs, ocean_mask, kappa_sq, block_ids):
@@ -309,9 +341,14 @@
             jax.ShapeDtypeStruct((count, rows, lanes), f32),
             jax.ShapeDtypeStruct((count, NB), f32),
         ),
-        in_specs=[vmem] * 4,
+        in_specs=[pl.BlockSpec(memory_space=pltpu.HBM)] * 4,
         out_specs=(vmem,) * 3,
         scratch_shapes=[
+            pltpu.VMEM((count, rows, lanes), jnp.int32),
+            pltpu.VMEM((rows, lanes), jnp.int32),
+            pltpu.VMEM((rows, lanes), f32),
+            pltpu.VMEM((rows, lanes), jnp.int32),
+            pltpu.VMEM((rows * NB, lanes), jnp.bfloat16),
             pltpu.VMEM((count + 1, ext, lanes), f32),
             pltpu.VMEM((2, ext, lanes), f32),
             pltpu.VMEM((rows, lanes), f32),
@@ -324,10 +361,11 @@
             pltpu.VMEM((3, count, lanes), f32),
             pltpu.VMEM((nlat, count, lanes), f32),
             pltpu.VMEM((nlon, count, lanes), f32),
-            pltpu.VMEM((nlat, count, lanes), f32),
-            pltpu.VMEM((nlon, count, lanes), f32),
-            pltpu.SemaphoreType.DMA((6,)),
-            pltpu.SemaphoreType.DMA((6,)),
+            pltpu.VMEM((nlat, 3 * count // 2, lanes), f32),
+            pltpu.VMEM((nlon, count // 2, lanes), f32),
+            pltpu.SemaphoreType.DMA((4,)),
+            pltpu.SemaphoreType.DMA((8,)),
+            pltpu.SemaphoreType.DMA((8,)),
             pltpu.SemaphoreType.DMA((2, nlat - 1)),
             pltpu.SemaphoreType.DMA((2, nlat - 1)),
             pltpu.SemaphoreType.DMA((2, nlon - 1)),

time: 43.4 us -> 41 us (0.945)
  Pallas kernels: 36.2 us -> 33.8 us
    pallas_call x1, Pallas kernels: 36.2 us -> 33.8 us  [per_device(): pl.pallas_call(functools.partial(kernel, nlat, nlon), out_shape=(jax.Shap...]
where the time goes in v2:
time: 41 us; the launch traced here: 40.7 us
  Pallas kernels  33.8 us (82%)
  local copies, waits for them, and re-layouts  6.27 us (15%)
  between operations  0.65 us (2%)
    pallas_call x1, Pallas kernels, per_device(): pl.pallas_call(functools.partial(kernel, nlat, nlon), out_shape=(jax.Shap...  33.8 us
    unnamed x11, local copies, waits for them, and re-layouts  6.27 us

profile of v2, /device:TPU:0, one launch (start us, length us, event | category | flops | bytes accessed | tf_op | source)
XLA Modules:
  0.0 40.7 jit_solution(7686608008001258927)
XLA Ops:
  0.6 0.0 copy-start
  0.6 1.2 %copy-done = s32[16,128,128]{2,1,0:T(8,128)S(1)} copy-done((s32[16,128,128]{2,1,0:T(8,128)S(1)}, s32[16,128,128]{2,1,0:T(8,128)}, u32[]{:S(2)}) %copy-start) | copy-done | bytes 1048600
  1.9 0.0 copy-start.1
  1.9 0.8 %copy-done.1 = s32[128,128]{1,0:T(8,128)S(1)} copy-done((s32[128,128]{1,0:T(8,128)S(1)}, s32[128,128]{1,0:T(8,128)}, u32[]{:S(2)}) %copy-start.1) | copy-done | bytes 65560
  2.7 0.0 copy-start.2
  2.7 0.8 %copy-done.2 = f32[128,128]{1,0:T(8,128)S(1)} copy-done((f32[128,128]{1,0:T(8,128)S(1)}, f32[128,128]{1,0:T(8,128)}, u32[]{:S(2)}) %copy-start.2) | copy-done | bytes 65560
  3.5 0.0 copy-start.3
  3.5 0.8 %copy-done.3 = s32[128,128]{1,0:T(8,128)S(1)} copy-done((s32[128,128]{1,0:T(8,128)S(1)}, s32[128,128]{1,0:T(8,128)}, u32[]{:S(2)}) %copy-start.3) | copy-done | bytes 65560
  4.4 33.8 %shard_map.67 = (f32[16,128,128]{2,1,0:T(8,128)S(1)}, f32[16,128,128]{2,1,0:T(8,128)S(1)}, f32[16,64]{1,0:T(8,128)S(1)}) custom-call(s32[16,128,128]{2,1,0:T(8,128)S(1)} %copy-done, s32[128,128]{1,0:T(8,128)S(1)} %copy-done.1, f32[128,128]{1,0:T(8,128)S(1)} %copy-done.2, s32[128,128]{1,0:T(8,128)S(1)} %copy-done.3), custom_call_target="tpu_custom_call" | custom-call | tf_op jit(solution)/shard_map/pallas_call | solution.py:337
  38.2 1.0 %copy.10 = f32[16,128,128]{2,1,0:T(8,128)} copy(f32[16,128,128]{2,1,0:T(8,128)S(1)} %get-tuple-element.6) | data formatting | bytes 2097152
  39.2 1.0 %copy.11 = f32[16,128,128]{2,1,0:T(8,128)} copy(f32[16,128,128]{2,1,0:T(8,128)S(1)} %get-tuple-element.7) | data formatting | bytes 2097152
  40.1 0.6 %copy.12 = f32[16,64]{1,0:T(8,128)} copy(f32[16,64]{1,0:T(8,128)S(1)} %get-tuple-element.8) | data formatting | bytes 8192
Async XLA Ops:
  0.6 1.2 %copy-start = (s32[16,128,128]{2,1,0:T(8,128)S(1)}, s32[16,128,128]{2,1,0:T(8,128)}, u32[]{:S(2)}) copy-start(s32[16,128,128]{2,1,0:T(8,128)} %signs_in.1) | copy-start | bytes 3145732
  1.9 0.8 %copy-start.1 = (s32[128,128]{1,0:T(8,128)S(1)}, s32[128,128]{1,0:T(8,128)}, u32[]{:S(2)}) copy-start(s32[128,128]{1,0:T(8,128)} %mask_in.1) | copy-start | bytes 196612
  2.7 0.8 %copy-start.2 = (f32[128,128]{1,0:T(8,128)S(1)}, f32[128,128]{1,0:T(8,128)}, u32[]{:S(2)}) copy-start(f32[128,128]{1,0:T(8,128)} %kappa_in.1) | copy-start | bytes 196612
  3.5 0.8 %copy-start.3 = (s32[128,128]{1,0:T(8,128)S(1)}, s32[128,128]{1,0:T(8,128)}, u32[]{:S(2)}) copy-start(s32[128,128]{1,0:T(8,128)} %ids_in.1) | copy-start | bytes 196612

commit v3 on v2

--- a/solution.py
+++ b/solution.py
@@ -38,10 +38,10 @@
 
 
 def kernel(
-    nlat, nlon, signs_in, mask_in, kappa_in, ids_in, solved, trace, traces,
-    signs, mask, kappa, ids, hits, planes, halo, left_edge, right_edge, coef, work, kept, terms, dots, ys,
+    nlat, nlon, signs_in, mask_in, kappa_in, ids_in, solved_out, trace_out, traces,
+    solved, trace, signs, mask, kappa, ids, hits, planes, halo, left_edge, right_edge, coef, work, kept, terms, dots, ys,
     gram_lat, gram_lon, sums_lat, sums_lon,
-    load_done, halo_send, halo_recv, lat_send, lat_recv, lon_send, lon_recv,
+    load_done, store_done, halo_send, halo_recv, lat_send, lat_recv, lon_send, lon_recv,
 ):
     loads = [
         pltpu.make_async_copy(src, dst, load_done.at[k])
@@ -323,10 +323,19 @@
         trace[p] = y0 * t[0] + y1 * t[1] + y2 * t[2]
         return carry
 
-    lax.fori_loop(0, count, finish, 0)
+    stores = []
+    part = count // 4
+    for k in range(4):
+        lax.fori_loop(k * part, (k + 1) * part, finish, 0)
+        at = pl.ds(k * part, part)
+        for j, (src, dst) in enumerate(((solved, solved_out), (trace, trace_out))):
+            stores.append(pltpu.make_async_copy(src.at[at], dst.at[at], store_done.at[k, j]))
+            stores[-1].start()
     total = gather(sums_lon, nlon, sent)
     total = jnp.concatenate([total[:, :NB], total[:, NB:]], axis=0)
     traces[...] = total / jnp.float32(rows * lanes * nlat * nlon // NB)
+    for store in stores:
+        store.wait()
 
 
 def per_device(nlat, nlon, probe_signs, ocean_mask, kappa_sq, block_ids):
@@ -342,8 +351,10 @@
             jax.ShapeDtypeStruct((count, NB), f32),
         ),
         in_specs=[pl.BlockSpec(memory_space=pltpu.HBM)] * 4,
-        out_specs=(vmem,) * 3,
+        out_specs=(pl.BlockSpec(memory_space=pltpu.HBM),) * 2 + (vmem,),
         scratch_shapes=[
+            pltpu.VMEM((count, rows, lanes), f32),
+            pltpu.VMEM((count, rows, lanes), f32),
             pltpu.VMEM((count, rows, lanes), jnp.int32),
             pltpu.VMEM((rows, lanes), jnp.int32),
             pltpu.VMEM((rows, lanes), f32),
@@ -364,6 +375,7 @@
             pltpu.VMEM((nlat, 3 * count // 2, lanes), f32),
             pltpu.VMEM((nlon, count // 2, lanes), f32),
             pltpu.SemaphoreType.DMA((4,)),
+            pltpu.SemaphoreType.DMA((4, 2)),
             pltpu.SemaphoreType.DMA((8,)),
             pltpu.SemaphoreType.DMA((8,)),
             pltpu.SemaphoreType.DMA((2, nlat - 1)),
@@ -372,7 +384,7 @@
             pltpu.SemaphoreType.DMA((2, nlon - 1)),
         ],
         compiler_params=pltpu.CompilerParams(
-            collective_id=0, has_side_effects=True, vmem_limit_bytes=40 * 1024 * 1024),
+            collective_id=0, has_side_effects=True, vmem_limit_bytes=64 * 1024 * 1024),
     )(probe_signs, ocean_mask, kappa_sq, block_ids)
 
 

time: 41 us -> 39.1 us (0.954)
  local copies, waits for them, and re-layouts: 6.27 us -> 3.96 us
  Pallas kernels: 33.8 us -> 34.3 us
    unnamed x11 -> x7, local copies, waits for them, and re-layouts: 6.27 us -> 3.96 us
    pallas_call x1, Pallas kernels: 33.8 us -> 34.3 us  [per_device(): pl.pallas_call(functools.partial(kernel, nlat, nlon), out_shape=(jax.Shap...]
where the time goes in v3:
time: 39.1 us; the launch traced here: 39 us
  Pallas kernels  34.3 us (88%)
  local copies, waits for them, and re-layouts  3.96 us (10%)
  between operations  0.65 us (2%)
    pallas_call x1, Pallas kernels, per_device(): pl.pallas_call(functools.partial(kernel, nlat, nlon), out_shape=(jax.Shap...  34.3 us
    unnamed x7, local copies, waits for them, and re-layouts  3.96 us

profile of v3, /device:TPU:0, one launch (start us, length us, event | category | flops | bytes accessed | tf_op | source)
XLA Modules:
  0.0 39.0 jit_solution(15243181178572204023)
XLA Ops:
  0.6 34.3 %shard_map.67 = (f32[16,128,128]{2,1,0:T(8,128)}, f32[16,128,128]{2,1,0:T(8,128)}, f32[16,64]{1,0:T(8,128)}) custom-call(s32[16,128,128]{2,1,0:T(8,128)} %signs_in.1, s32[128,128]{1,0:T(8,128)} %mask_in.1, f32[128,128]{1,0:T(8,128)} %kappa_in.1, s32[128,128]{1,0:T(8,128)} %ids_in.1), custom_call_target="tpu_custom_call" | custom-call | tf_op jit(solution)/shard_map/pallas_call | solution.py:346
  35.0 0.0 copy-start
  35.0 2.4 %copy.10 = f32[16,128,128]{2,1,0:T(8,128)} copy(f32[16,128,128]{2,1,0:T(8,128)} %get-tuple-element.6) | data formatting | bytes 2097152
  37.4 0.0 copy-done
  37.4 0.0 copy-start.1
  37.4 1.0 %copy.11 = f32[16,128,128]{2,1,0:T(8,128)} copy(f32[16,128,128]{2,1,0:T(8,128)S(1)} %copy-done) | data formatting | bytes 2097152
  38.4 0.0 copy-done.1
  38.4 0.6 %copy.12 = f32[16,64]{1,0:T(8,128)} copy(f32[16,64]{1,0:T(8,128)S(1)} %copy-done.1) | data formatting | bytes 8192
Async XLA Ops:
  35.0 2.4 %copy-start = (f32[16,128,128]{2,1,0:T(8,128)S(1)}, f32[16,128,128]{2,1,0:T(8,128)}, u32[]{:S(2)}) copy-start(f32[16,128,128]{2,1,0:T(8,128)} %get-tuple-element.7) | copy-start | bytes 3145732
  37.4 1.0 %copy-start.1 = (f32[16,64]{1,0:T(8,128)S(1)}, f32[16,64]{1,0:T(8,128)}, u32[]{:S(2)}) copy-start(f32[16,64]{1,0:T(8,128)} %get-tuple-element.8) | copy-start | bytes 12292

commit v4 on v3

--- a/solution.py
+++ b/solution.py
@@ -13,6 +13,7 @@
 SHIFT = 0.4
 FLOOR = 1e-6
 CHUNK = 48
+GROUP = 4
 MESH = pl.DeviceIdType.MESH
 
 
@@ -219,21 +220,30 @@
         o = a + PAD
         return work[src, 0, o:o + n, :], work[src, 1, o:o + n, :]
 
-    def probe(p, carry):
-        for a, n in chunks:
-            put(0, a, n, (planes[p, a:a + n, :], unpack(p, a, n)))
+    def probes(group, carry):
+        each = [(u, group * GROUP + u) for u in range(GROUP)]
+        for u, p in each:
+            for a, n in chunks:
+                put(5 * u, a, n, (planes[p, a:a + n, :], unpack(p, a, n)))
         for k in range(3):
+            for u, p in each:
+                for a, n in chunks:
+                    put(5 * u + k + 1, a, n, apply(5 * u + k, a, n, True))
+        for u, p in each:
             for a, n in chunks:
-                put(k + 1, a, n, apply(k, a, n, True))
-        for a, n in chunks:
-            m, h = apply(3, a, n, True)
-            m_old, h_old = get(2, a, n)
-            put(4, a, n, (m - SHIFT * m_old, h - SHIFT * h_old))
+                m, h = apply(5 * u + 3, a, n, True)
+                m_old, h_old = get(5 * u + 2, a, n)
+                put(5 * u + 4, a, n, (m - SHIFT * m_old, h - SHIFT * h_old))
+        for u, p in each:
+            last_step(u, p)
+        return carry
+
+    def last_step(u, p):
         part = [jnp.zeros((8, lanes), jnp.float32) for _ in range(7)]
         step = 32
         for a in range(0, rows, step):
-            w2, _ = apply(4, a + PAD, step, False)
-            v0, w0, v1, w1, v2 = (get(k, a + PAD, step)[0] for k in range(5))
+            w2, _ = apply(5 * u + 4, a + PAD, step, False)
+            v0, w0, v1, w1, v2 = (get(5 * u + k, a + PAD, step)[0] for k in range(5))
             k = kappa[a:a + step, :]
             kept[0, p, a:a + step, :] = v1
             kept[1, p, a:a + step, :] = v2
@@ -247,9 +257,8 @@
                     part[j] = part[j] + xy[i:i + 8]
         for j in range(7):
             dots[j, pl.ds(p, 1), :] = jnp.sum(part[j], axis=0, keepdims=True)
-        return carry
-
-    lax.fori_loop(0, count, probe, 0)
+
+    lax.fori_loop(0, count // GROUP, probes, 0)
 
     def share(buf, mine, n, send, recv, axis):
         copies = []
@@ -295,10 +304,10 @@
             (((1,), (1,)), ((), ())), preferred_element_type=jnp.float32)
 
     acc = jnp.zeros((6 * count, NB), jnp.float32)
-    acc = lax.fori_loop(0, rows // 4, sums, acc, unroll=4)
+    acc = lax.fori_loop(0, rows // 4, sums, acc, unroll=8)
     gram_lon[lon] = gather(gram_lat, nlat, sent)
     sent = share(gram_lon, lon, nlon, lon_send.at[0], lon_recv.at[0], 1)
-    acc = lax.fori_loop(rows // 4, rows // 2, sums, acc, unroll=4)
+    acc = lax.fori_loop(rows // 4, rows // 2, sums, acc, unroll=8)
     half = 3 * count // 2
     acc = acc[:3 * count] + acc[3 * count:]
     sums_lat[lat] = jnp.concatenate([acc[:half], acc[half:]], axis=1)
@@ -365,7 +374,7 @@
             pltpu.VMEM((rows, lanes), f32),
             pltpu.VMEM((rows, lanes), f32),
             pltpu.VMEM((2, 2, ext, lanes), f32),
-            pltpu.VMEM((5, 2, ext + 2 * PAD, lanes), f32),
+            pltpu.VMEM((5 * GROUP, 2, ext + 2 * PAD, lanes), f32),
             pltpu.VMEM((2, count, rows, lanes), f32),
             pltpu.VMEM((3 * count * rows, lanes), f32),
             pltpu.VMEM((8, count, lanes), f32),

time: 39.1 us -> 37 us (0.946)
  Pallas kernels: 34.3 us -> 32.2 us
    pallas_call x1, Pallas kernels: 34.3 us -> 32.2 us  [per_device(): pl.pallas_call(functools.partial(kernel, nlat, nlon), out_shape=(jax.Shap...]
where the time goes in v4:
time: 37 us; the launch traced here: 36.8 us
  Pallas kernels  32.2 us (87%)
  local copies, waits for them, and re-layouts  3.96 us (11%)
  between operations  0.65 us (2%)
    pallas_call x1, Pallas kernels, per_device(): pl.pallas_call(functools.partial(kernel, nlat, nlon), out_shape=(jax.Shap...  32.2 us
    unnamed x7, local copies, waits for them, and re-layouts  3.96 us

profile of v4, /device:TPU:0, one launch (start us, length us, event | category | flops | bytes accessed | tf_op | source)
XLA Modules:
  0.0 36.8 jit_solution(6229011892686549970)
XLA Ops:
  0.6 32.2 %shard_map.67 = (f32[16,128,128]{2,1,0:T(8,128)}, f32[16,128,128]{2,1,0:T(8,128)}, f32[16,64]{1,0:T(8,128)}) custom-call(s32[16,128,128]{2,1,0:T(8,128)} %signs_in.1, s32[128,128]{1,0:T(8,128)} %mask_in.1, f32[128,128]{1,0:T(8,128)} %kappa_in.1, s32[128,128]{1,0:T(8,128)} %ids_in.1), custom_call_target="tpu_custom_call" | custom-call | tf_op jit(solution)/shard_map/pallas_call | solution.py:355
  32.9 0.0 copy-start
  32.9 2.4 %copy.10 = f32[16,128,128]{2,1,0:T(8,128)} copy(f32[16,128,128]{2,1,0:T(8,128)} %get-tuple-element.6) | data formatting | bytes 2097152
  35.3 0.0 copy-done
  35.3 0.0 copy-start.1
  35.3 1.0 %copy.11 = f32[16,128,128]{2,1,0:T(8,128)} copy(f32[16,128,128]{2,1,0:T(8,128)S(1)} %copy-done) | data formatting | bytes 2097152
  36.2 0.0 copy-done.1
  36.2 0.6 %copy.12 = f32[16,64]{1,0:T(8,128)} copy(f32[16,64]{1,0:T(8,128)S(1)} %copy-done.1) | data formatting | bytes 8192
Async XLA Ops:
  32.9 2.4 %copy-start = (f32[16,128,128]{2,1,0:T(8,128)S(1)}, f32[16,128,128]{2,1,0:T(8,128)}, u32[]{:S(2)}) copy-start(f32[16,128,128]{2,1,0:T(8,128)} %get-tuple-element.7) | copy-start | bytes 3145732
  35.3 1.0 %copy-start.1 = (f32[16,64]{1,0:T(8,128)S(1)}, f32[16,64]{1,0:T(8,128)}, u32[]{:S(2)}) copy-start(f32[16,64]{1,0:T(8,128)} %get-tuple-element.8) | copy-start | bytes 12292

commit v5 on v4

--- a/solution.py
+++ b/solution.py
@@ -177,15 +177,29 @@
 
     chunks = [(a, min(CHUNK, ext - a)) for a in range(0, ext, CHUNK)]
 
-    def unpack(p, a, n):
-        left = pltpu.roll(halo[0, a:a + n, :], lax.rem(2 * lanes - EDGE - EDGE * p, lanes), 1)
-        right = pltpu.roll(halo[1, a:a + n, :], lax.rem(2 * lanes - EDGE * p, lanes), 1)
-        return jnp.where(lane < EDGE, right, jnp.where(lane >= lanes - EDGE, left, 0.0))
+    width = lanes // GROUP
+    spot = lax.rem(lane, width)
+
+    def strip(pairs, a, n):
+        out = jnp.zeros((n, lanes), jnp.float32)
+        for u, p in pairs:
+            x = planes[p, a:a + n, :]
+            pieces = (
+                (x, width * u + 8, 0, 8),
+                (halo[1, a:a + n, :], lax.rem(width * u + 8 - EDGE * p + 2 * lanes, lanes), 8, 15),
+                (halo[0, a:a + n, :], lax.rem(width * u + 17 - EDGE * p + 2 * lanes, lanes), 17, 24),
+                (x, (width * u + 24) % lanes, 24, 32),
+            )
+            for source, shift, lo, hi in pieces:
+                here = (lane >= width * u + lo) & (lane < width * u + hi)
+                out = jnp.where(here, pltpu.roll(source, shift, 1), out)
+        return out
 
     for a, n in chunks:
         for s in range(2):
             if s:
-                ocean, k = unpack(0, a, n), unpack(count, a, n)
+                ocean = strip([(u, 0) for u in range(GROUP)], a, n)
+                k = strip([(u, count) for u in range(GROUP)], a, n)
             else:
                 ocean, k = planes[0, a:a + n, :], planes[count, a:a + n, :]
             ocean = ocean * ocean
@@ -194,46 +208,49 @@
 
     at_first, at_last = lane == 0, lane == lanes - 1
 
-    def apply(src, a, n, wide):
+    def vertical(src, s, o, n):
+        return work[src, s, o - 1:o + n - 1, :] + work[src, s, o + 1:o + n + 1, :]
+
+    def apply(u, k, a, n):
+        o, src = a + PAD, 5 * u + k
+        m = work[src, 0, o:o + n, :]
+        e = pltpu.roll(work[5 + k, 1, o:o + n, :], (2 * lanes - width * u - 23) % lanes, 1)
+        total = vertical(src, 0, o, n) + jnp.where(at_first, e, pltpu.roll(m, 1, 1))
+        total = total + jnp.where(at_last, e, pltpu.roll(m, lanes - 1, 1))
+        return coef[0, 0, a:a + n, :] * m - coef[1, 0, a:a + n, :] * total
+
+    def apply_strip(k, a, n):
         o = a + PAD
-        m, h = work[src, 0, o:o + n, :], work[src, 1, o:o + n, :]
-        m_right, h_right = pltpu.roll(m, 1, 1), pltpu.roll(h, 1, 1)
-        m_left, h_left = pltpu.roll(m, lanes - 1, 1), pltpu.roll(h, lanes - 1, 1)
-
-        def one(s, x, a_side, b_side):
-            total = work[src, s, o - 1:o + n - 1, :] + work[src, s, o + 1:o + n + 1, :]
-            total = total + a_side + b_side
-            return coef[0, s, a:a + n, :] * x - coef[1, s, a:a + n, :] * total
-
-        out = one(0, m, jnp.where(at_first, h_right, m_right), jnp.where(at_last, h_left, m_left))
-        if not wide:
-            return out, None
-        return out, one(
-            1, h, jnp.where(at_first, m_right, h_right), jnp.where(at_last, m_left, h_left))
-
-    def put(dst, a, n, pair):
+        x = work[k, 1, o:o + n, :]
+        total = vertical(k, 1, o, n) + pltpu.roll(x, 1, 1) + pltpu.roll(x, lanes - 1, 1)
+        return coef[0, 1, a:a + n, :] * x - coef[1, 1, a:a + n, :] * total
+
+    def put_strip(k, a, n, x):
         o = a + PAD
-        work[dst, 0, o:o + n, :] = pair[0]
-        work[dst, 1, o:o + n, :] = pair[1]
+        work[k, 1, o:o + n, :] = x
+        work[5 + k, 1, o:o + n, :] = jnp.where(spot == 23, x, pltpu.roll(x, 14, 1))
 
     def get(src, a, n):
-        o = a + PAD
-        return work[src, 0, o:o + n, :], work[src, 1, o:o + n, :]
+        return work[src, 0, a + PAD:a + PAD + n, :]
 
     def probes(group, carry):
         each = [(u, group * GROUP + u) for u in range(GROUP)]
-        for u, p in each:
+        for a, n in chunks:
+            put_strip(0, a, n, strip(each, a, n))
+            for u, p in each:
+                work[5 * u, 0, a + PAD:a + PAD + n, :] = planes[p, a:a + n, :]
+        for k in range(4):
             for a, n in chunks:
-                put(5 * u, a, n, (planes[p, a:a + n, :], unpack(p, a, n)))
-        for k in range(3):
+                x = apply_strip(k, a, n)
+                if k == 3:
+                    x = x - SHIFT * work[2, 1, a + PAD:a + PAD + n, :]
+                put_strip(k + 1, a, n, x)
             for u, p in each:
                 for a, n in chunks:
-                    put(5 * u + k + 1, a, n, apply(5 * u + k, a, n, True))
-        for u, p in each:
-            for a, n in chunks:
-                m, h = apply(5 * u + 3, a, n, True)
-                m_old, h_old = get(5 * u + 2, a, n)
-                put(5 * u + 4, a, n, (m - SHIFT * m_old, h - SHIFT * h_old))
+                    x = apply(u, k, a, n)
+                    if k == 3:
+                        x = x - SHIFT * get(5 * u + 2, a, n)
+                    work[5 * u + k + 1, 0, a + PAD:a + PAD + n, :] = x
         for u, p in each:
             last_step(u, p)
         return carry
@@ -242,8 +259,8 @@
         part = [jnp.zeros((8, lanes), jnp.float32) for _ in range(7)]
         step = 32
         for a in range(0, rows, step):
-            w2, _ = apply(5 * u + 4, a + PAD, step, False)
-            v0, w0, v1, w1, v2 = (get(5 * u + k, a + PAD, step)[0] for k in range(5))
+            w2 = apply(u, 4, a + PAD, step)
+            v0, w0, v1, w1, v2 = (get(5 * u + k, a + PAD, step) for k in range(5))
             k = kappa[a:a + step, :]
             kept[0, p, a:a + step, :] = v1
             kept[1, p, a:a + step, :] = v2

time: 37 us -> 41.5 us (1.12)
  Pallas kernels: 32.2 us -> 36.7 us
    pallas_call x1, Pallas kernels: 32.2 us -> 36.7 us  [per_device(): pl.pallas_call(functools.partial(kernel, nlat, nlon), out_shape=(jax.Shap...]
where the time goes in v5:
time: 41.5 us; the launch traced here: 41.3 us
  Pallas kernels  36.7 us (88%)
  local copies, waits for them, and re-layouts  3.96 us (10%)
  between operations  0.65 us (2%)
    pallas_call x1, Pallas kernels, per_device(): pl.pallas_call(functools.partial(kernel, nlat, nlon), out_shape=(jax.Shap...  36.7 us
    unnamed x7, local copies, waits for them, and re-layouts  3.96 us

profile of v5, /device:TPU:0, one launch (start us, length us, event | category | flops | bytes accessed | tf_op | source)
XLA Modules:
  0.0 41.3 jit_solution(12009065580605832917)
XLA Ops:
  0.6 36.7 %shard_map.67 = (f32[16,128,128]{2,1,0:T(8,128)}, f32[16,128,128]{2,1,0:T(8,128)}, f32[16,64]{1,0:T(8,128)}) custom-call(s32[16,128,128]{2,1,0:T(8,128)} %signs_in.1, s32[128,128]{1,0:T(8,128)} %mask_in.1, f32[128,128]{1,0:T(8,128)} %kappa_in.1, s32[128,128]{1,0:T(8,128)} %ids_in.1), custom_call_target="tpu_custom_call" | custom-call | tf_op jit(solution)/shard_map/pallas_call | solution.py:372
  37.4 0.0 copy-start
  37.4 2.4 %copy.10 = f32[16,128,128]{2,1,0:T(8,128)} copy(f32[16,128,128]{2,1,0:T(8,128)} %get-tuple-element.6) | data formatting | bytes 2097152
  39.8 0.0 copy-done
  39.8 0.0 copy-start.1
  39.8 1.0 %copy.11 = f32[16,128,128]{2,1,0:T(8,128)} copy(f32[16,128,128]{2,1,0:T(8,128)S(1)} %copy-done) | data formatting | bytes 2097152
  40.7 0.0 copy-done.1
  40.7 0.6 %copy.12 = f32[16,64]{1,0:T(8,128)} copy(f32[16,64]{1,0:T(8,128)S(1)} %copy-done.1) | data formatting | bytes 8192
Async XLA Ops:
  37.4 2.4 %copy-start = (f32[16,128,128]{2,1,0:T(8,128)S(1)}, f32[16,128,128]{2,1,0:T(8,128)}, u32[]{:S(2)}) copy-start(f32[16,128,128]{2,1,0:T(8,128)} %get-tuple-element.7) | copy-start | bytes 3145732
  39.8 1.0 %copy-start.1 = (f32[16,64]{1,0:T(8,128)S(1)}, f32[16,64]{1,0:T(8,128)}, u32[]{:S(2)}) copy-start(f32[16,64]{1,0:T(8,128)} %get-tuple-element.8) | copy-start | bytes 12292

commit v6 on v4

--- a/solution.py
+++ b/solution.py
@@ -12,7 +12,7 @@
 PAD = 8
 SHIFT = 0.4
 FLOOR = 1e-6
-CHUNK = 48
+CHUNK = 24
 GROUP = 4
 MESH = pl.DeviceIdType.MESH
 

time: 37 us -> 37.1 us (level)
  no operation moved by 1% of the time
where the time goes in v6:
time: 37.1 us; the launch traced here: 36.9 us
  Pallas kernels  32.3 us (87%)
  local copies, waits for them, and re-layouts  3.96 us (11%)
  between operations  0.65 us (2%)
    pallas_call x1, Pallas kernels, per_device(): pl.pallas_call(functools.partial(kernel, nlat, nlon), out_shape=(jax.Shap...  32.3 us
    unnamed x7, local copies, waits for them, and re-layouts  3.96 us

profile of v6, /device:TPU:0, one launch (start us, length us, event | category | flops | bytes accessed | tf_op | source)
XLA Modules:
  0.0 36.9 jit_solution(11989582273137636722)
XLA Ops:
  0.6 32.3 %shard_map.67 = (f32[16,128,128]{2,1,0:T(8,128)}, f32[16,128,128]{2,1,0:T(8,128)}, f32[16,64]{1,0:T(8,128)}) custom-call(s32[16,128,128]{2,1,0:T(8,128)} %signs_in.1, s32[128,128]{1,0:T(8,128)} %mask_in.1, f32[128,128]{1,0:T(8,128)} %kappa_in.1, s32[128,128]{1,0:T(8,128)} %ids_in.1), custom_call_target="tpu_custom_call" | custom-call | tf_op jit(solution)/shard_map/pallas_call | solution.py:355
  32.9 0.0 copy-start
  33.0 2.4 %copy.10 = f32[16,128,128]{2,1,0:T(8,128)} copy(f32[16,128,128]{2,1,0:T(8,128)} %get-tuple-element.6) | data formatting | bytes 2097152
  35.3 0.0 copy-done
  35.3 0.0 copy-start.1
  35.3 1.0 %copy.11 = f32[16,128,128]{2,1,0:T(8,128)} copy(f32[16,128,128]{2,1,0:T(8,128)S(1)} %copy-done) | data formatting | bytes 2097152
  36.3 0.0 copy-done.1
  36.3 0.6 %copy.12 = f32[16,64]{1,0:T(8,128)} copy(f32[16,64]{1,0:T(8,128)S(1)} %copy-done.1) | data formatting | bytes 8192
Async XLA Ops:
  32.9 2.4 %copy-start = (f32[16,128,128]{2,1,0:T(8,128)S(1)}, f32[16,128,128]{2,1,0:T(8,128)}, u32[]{:S(2)}) copy-start(f32[16,128,128]{2,1,0:T(8,128)} %get-tuple-element.7) | copy-start | bytes 3145732
  35.3 1.0 %copy-start.1 = (f32[16,64]{1,0:T(8,128)S(1)}, f32[16,64]{1,0:T(8,128)}, u32[]{:S(2)}) copy-start(f32[16,64]{1,0:T(8,128)} %get-tuple-element.8) | copy-start | bytes 12292
